TPU v7x, 512 devices: a whole 4x4x16 slice. The times are simulated.
512 devices in a mesh: dom: 64 (over x, z), head: 8 (over y, core).
Axes of the slice: x: 4, y: 4, z: 16, core: 2. Of those that a mesh axis runs over, the one named last changes fastest.
Arguments:
- node_feats: bfloat16 [65536, 512], P(('dom', 'head')), may hold values from -6 to 6
- norm_gain: float32 [512], replicated, may hold values from 0.25 to 1.75
- w_qkv: bfloat16 [512, 1536], P(None, 'head'), may hold values from -1 to 1
- w_out: bfloat16 [512, 512], replicated, may hold values from -0.25 to 0.25
- rand_feat: float32 [8, 64, 256], P('head'), may hold values from -6 to 6
- temper: float32 [8], P('head'), may hold values from 1 to 6
- edge_src: int32 [512, 6], P('dom'), may hold values from 0 to 511, as said below
- edge_count: int32 [512], P('dom'), may hold values from 1 to 6, as said below
- block_fill: int32 [512], replicated, may hold values from 32 to 128, as said below
Outputs:
- update: bfloat16 [65536, 512], P(('dom', 'head'))
Inputs may be any that keep to these rules, and one draw needn't show every extreme that they name: `edge_src`: destination block b lies in partition p = b // 8; each of its source blocks lies in partition p - 1, p or p + 1; slot 0 holds b itself, and slots at or beyond edge_count[b] hold b. `edge_count`: every block of some partition uses all 6 slots. `block_fill`: block 0 is full.
All inputs are finite; a program needn't handle non-finite values.
Results may differ from a plain program's by a relative error of at most 0.012.
The roundings to bfloat16 on the way count: a program that leaves them out, or rounds other values in their place, can miss the bound.
Values may be sent and summed in bfloat16 or wider, within the bound.
A program may use at most 64 MiB of HBM per device.

v0:
```python
import math

import jax
import jax.numpy as jnp
from jax import lax
from jax.sharding import PartitionSpec as P

BLK = 128


def padded(block, sides, width):
    for axis, dim in sides:
        count = lax.axis_size(axis)
        forward = [(i, i + 1) for i in range(count - 1)]
        backward = [(target, source) for source, target in forward]
        low = lax.ppermute(
            lax.slice_in_dim(block, block.shape[dim] - width, None, axis=dim), axis, forward
        )
        high = lax.ppermute(lax.slice_in_dim(block, 0, width, axis=dim), axis, backward)
        block = jnp.concatenate([low, block, high], axis=dim)
    return block


def layer_norm(rows, gain):
    widened = rows.astype(jnp.float32)
    centred = widened - jnp.mean(widened, axis=-1, keepdims=True)
    spread = jnp.mean(centred * centred, axis=-1, keepdims=True)
    return (centred * lax.rsqrt(spread + 1e-05) * gain).astype(jnp.bfloat16)


def features(rows, directions, temper):
    head_dim = rows.shape[-1]
    scaled = rows.astype(jnp.float32) * (jnp.sqrt(temper)[None, :, None] * head_dim ** (-0.25))
    lifted = jnp.einsum("nhd,hdm->nhm", scaled, directions, precision=lax.Precision.HIGHEST)
    return jnp.exp(
        lifted - 0.5 * jnp.sum(scaled * scaled, axis=-1, keepdims=True)
    ) * directions.shape[2] ** (-0.5)


def shards(
    node_feats, norm_gain, w_qkv, w_out, rand_feat, temper, edge_src, edge_count, block_fill
):
    groups = lax.axis_size("head")
    heads_here = rand_feat.shape[0]
    head_dim = rand_feat.shape[1]
    part_rows = node_feats.shape[0] * groups
    blocks = part_rows // BLK
    slots = edge_src.shape[1]
    domain = lax.axis_index("dom")
    normed = layer_norm(node_feats, norm_gain)
    qkv = jnp.dot(
        lax.all_gather(normed, "head", axis=0, tiled=True),
        w_qkv,
        preferred_element_type=jnp.float32,
    ).astype(jnp.bfloat16)
    split = qkv.reshape(part_rows, heads_here, 3, head_dim)
    queries = split[:, :, 0]
    own_fill = lax.dynamic_slice_in_dim(block_fill, domain * blocks, blocks)
    lanes = lax.broadcasted_iota(jnp.int32, (blocks, BLK), 1)
    valid = (lanes < own_fill[:, None]).astype(jnp.float32).reshape(part_rows)
    phi_keys = features(split[:, :, 1], rand_feat, temper) * valid[:, None, None]
    partial_sum = jnp.einsum(
        "nhm,nhe->hme",
        phi_keys,
        split[:, :, 2].astype(jnp.float32),
        precision=lax.Precision.HIGHEST,
    )
    kernel_sum, key_total = lax.psum((partial_sum, jnp.sum(phi_keys, axis=0)), "dom")
    pairs = split[:, :, 1:].reshape(part_rows, heads_here * 2 * head_dim)
    widened = padded(pairs, (("dom", 0),), part_rows)
    kv_blocks = widened.reshape(3 * blocks, BLK, heads_here, 2, head_dim)
    key_blocks = kv_blocks[:, :, :, 0]
    value_blocks = kv_blocks[:, :, :, 1]
    local_src = edge_src - (domain - 1) * blocks
    scale = head_dim ** (-0.5)
    per_step = math.gcd(blocks, max(1, 8 // heads_here))
    turns = blocks // per_step
    width = slots * BLK
    q_steps = queries.reshape(turns, per_step, BLK, heads_here, head_dim)
    src_steps = local_src.reshape(turns, per_step, slots)
    id_steps = edge_src.reshape(turns, per_step, slots)
    count_steps = edge_count.reshape(turns, per_step)

    def attend_all(packed):
        q_part, src_part, id_part, count_part = packed
        keys = jnp.take(key_blocks, src_part, axis=0).reshape(per_step, width, heads_here, head_dim)
        values = jnp.take(value_blocks, src_part, axis=0).reshape(
            per_step, width, heads_here, head_dim
        )
        fills = jnp.take(block_fill, id_part)
        slot_ids = lax.broadcasted_iota(jnp.int32, (per_step, slots, BLK), 1)
        lane_ids = lax.broadcasted_iota(jnp.int32, (per_step, slots, BLK), 2)
        allowed = ((lane_ids < fills[:, :, None]) & (slot_ids < count_part[:, None, None])).reshape(
            per_step, width
        )
        scores = (
            jnp.einsum("bqhd,bkhd->bhqk", q_part, keys, preferred_element_type=jnp.float32) * scale
        )
        scores = jnp.where(allowed[:, None, None, :], scores, -1e30)
        row_max = jnp.max(scores, axis=3, keepdims=True)
        weights = jnp.exp(scores - row_max)
        total = jnp.sum(weights, axis=3)
        accum = jnp.einsum(
            "bhqk,bkhd->bqhd",
            weights.astype(jnp.bfloat16),
            values,
            preferred_element_type=jnp.float32,
        )
        return accum / jnp.transpose(total, (0, 2, 1))[..., None]

    local = lax.map(attend_all, (q_steps, src_steps, id_steps, count_steps))
    local = local.reshape(part_rows, heads_here, head_dim)
    phi_queries = features(queries, rand_feat, temper)
    numer = jnp.einsum("nhm,hme->nhe", phi_queries, kernel_sum, precision=lax.Precision.HIGHEST)
    denom = jnp.einsum("nhm,hm->nh", phi_queries, key_total, precision=lax.Precision.HIGHEST)
    mixed = (
        (local + numer / denom[..., None])
        .astype(jnp.bfloat16)
        .reshape(part_rows, heads_here * head_dim)
    )
    returned = lax.all_to_all(mixed, "head", split_axis=0, concat_axis=1, tiled=True)
    return jnp.dot(returned, w_out, preferred_element_type=jnp.float32).astype(jnp.bfloat16)


def solution(mesh):
    return jax.shard_map(
        shards,
        mesh=mesh,
        in_specs=(
            P(("dom", "head"), None),
            P(),
            P(None, "head"),
            P(),
            P("head", None, None),
            P("head"),
            P("dom", None),
            P("dom"),
            P(),
        ),
        out_specs=P(("dom", "head"), None),
        check_vma=False,
    )
```

profile of v0, /device:TPU:1, one launch (start us, length us, event | category | flops | bytes accessed | tf_op | source)
XLA Modules:
  0.0 337.9 jit_solution(1613953993842794324)
XLA Ops:
  6.5 0.0 all-gather.2.cloned.1.call-start
  6.6 1.1 convert_reduce_fusion
  7.7 1.1 fusion.31
  8.8 1.7 fusion.33
  10.5 0.0 all-gather.2.cloned.1.call-update
  10.5 0.0 all-reduce.2.cloned.1.call-start
  10.6 1.3 compare_and_fusion
  11.8 0.1 reshape.313
  11.9 0.7 compare_select_fusion.1
  12.6 0.1 reshape.298
  12.7 0.8 gather_fusion
  13.5 0.1 reshape.297
  13.6 0.1 copy.20
  14.4 0.1 dynamic_slice.14
  14.5 0.1 select_bitcast_fusion
  14.6 0.1 fusion.44
  14.6 33.0 %all-gather.2.cloned.1.call-done = bf16[1024,512]{1,0:T(8,128)(2,1)} async-done(((bf16[128,512]{1,0:T(8,128)(2,1)}), bf16[1024,512]{1,0:T(8,128)(2,1)}) %all-gather.2.cloned.1.call-update) | async-done | bytes 1048592 | tf_op jit(solution)/shard_map/all_gather | solution.py:52
  47.6 1.7 convolution_convert_fusion
  49.4 3.0 collective-permute-start
  52.4 1.3 collective-permute-start.1
  53.7 0.1 multiply_reduce_fusion
  53.9 1.3 fusion.48
  55.1 1.1 fusion.27
  56.2 1.1 fusion.12
  57.4 0.7 copy.30
  58.1 0.0 all-reduce.2.cloned.1.call-update
  58.1 117.4 %psum.15 = f32[256]{0:T(256)S(1)} all-reduce(f32[256]{0:T(256)S(1)} %get-tuple-element.43), channel_id=1, replica_groups=mesh['dom'=64,'head'=8] {'dom'}, use_global_device_ids=true, to_apply=%region_8.10 | all-reduce | flops 256 | bytes 2048 | tf_op jit(solution)/shard_map/psum | solution.py:68
  175.5 1.0 fusion.49
  176.5 0.0 collective-permute-done.1
  176.5 0.1 maximum_bitcast_fusion
  176.6 0.2 copy.29
  176.7 0.1 fusion.47
  176.8 0.2 copy_bitcast_fusion
  177.0 0.7 gather_fusion.1
  177.7 0.7 gather_fusion.2
  178.4 1.8 broadcast_select_fusion
  180.2 0.6 copy.22
  180.7 0.9 reshape.266
  181.6 1.7 copy.19
  183.3 1.8 reshape.264
  185.1 0.7 fusion
  185.8 0.9 fusion.1
  186.8 1.0 fusion.24
  187.7 0.2 copy.24
  187.9 120.0 %all-reduce.2.cloned.1.call-done = f32[256,64]{0,1:T(8,128)} async-done(((f32[256,64]{0,1:T(8,128)}), f32[256,64]{0,1:T(8,128)}) %all-reduce.2.cloned.1.call-update) | async-done | bytes 65552 | tf_op jit(solution)/shard_map/psum | solution.py:68
  307.9 2.0 fusion.20
  309.9 20.3 %all_to_all.19 = bf16[8,128,64]{1,2,0:T(8,128)(2,1)S(1)} all-to-all(bf16[8,128,64]{1,2,0:T(8,128)(2,1)S(1)} %copy.26), channel_id=1, replica_groups=mesh['dom'=64,'head'=8] {'head'}, dimensions={0} | all-to-all | bytes 262144 | tf_op jit(solution)/shard_map/all_to_all | solution.py:121
  330.2 0.9 convolution_convert_fusion.1
  (29 shorter events, 0.1 us)
Async XLA Ops:
  6.5 323.6 %copy-start = (bf16[512,512]{1,0:T(8,128)(2,1)S(1)}, bf16[512,512]{1,0:T(8,128)(2,1)}, u32[]{:S(2)}) copy-start(bf16[512,512]{1,0:T(8,128)(2,1)} %param.14) | copy-start | bytes 1572868
  6.5 7.1 %copy-start.6 = (s32[8,6]{1,0:T(8,128)S(1)}, s32[8,6]{1,0:T(8,128)}, u32[]{:S(2)}) copy-start(s32[8,6]{1,0:T(8,128)} %param.17) | copy-start | bytes 580
  6.5 6.2 %copy-start.1 = (s32[512]{0:T(512)S(1)}, s32[512]{0:T(512)}, u32[]{:S(2)}) copy-start(s32[512]{0:T(512)} %param.19) | copy-start | bytes 6148
  6.5 8.0 %copy-start.7 = (s32[8]{0:T(128)S(1)}, s32[8]{0:T(128)}, u32[]{:S(2)}) copy-start(s32[8]{0:T(128)} %param.18) | copy-start | bytes 100
  6.5 41.1 %copy-start.5 = (bf16[512,192]{0,1:T(8,128)(2,1)S(1)}, bf16[512,192]{0,1:T(8,128)(2,1)}, u32[]{:S(2)}) copy-start(bf16[512,192]{0,1:T(8,128)(2,1)} %param.13) | copy-start | bytes 589828
  6.5 41.1 %all-gather.2.cloned.1.call-start = ((), (), s32[]{:S(2)}) async-start(), calls=%async_computation.1 | async-start | bytes 1179648 | tf_op jit(solution)/shard_map/all_gather | solution.py:52
  10.5 297.3 %all-reduce.2.cloned.1.call-start = ((), (), s32[]{:S(2)}) async-start(), calls=%async_computation.2 | async-start | bytes 131072 | tf_op jit(solution)/shard_map/psum | solution.py:68
  12.7 41.1 %copy-start.4 = (f32[1,64,256]{2,1,0:T(8,128)S(1)}, f32[1,64,256]{2,1,0:T(8,128)}, u32[]{:S(2)}) copy-start(f32[1,64,256]{2,1,0:T(8,128)} %param.15) | copy-start | bytes 196612
  49.4 127.1 %collective-permute-start = (bf16[1024,128]{0,1:T(8,128)(2,1)S(1)}, bf16[1024,128]{0,1:T(8,128)(2,1)S(1)}, u32[]{:S(2)}, u32[]{:S(2)}) collective-permute-start(bf16[1024,128]{0,1:T(8,128)(2,1)S(1)} %bitcast.148), channel_id=1, source_target_pairs={{0,8},{8,16},{16,24},{24,32},{32,40},{40,48},{48,56},{56,64},{64,7... | collective-permute-start | bytes 786440 | tf_op jit(solution)/shard_map/ppermute | solution.py:16
  52.4 124.1 %collective-permute-start.1 = (bf16[1024,128]{0,1:T(8,128)(2,1)S(1)}, bf16[1024,128]{0,1:T(8,128)(2,1)S(1)}, u32[]{:S(2)}, u32[]{:S(2)}) collective-permute-start(bf16[1024,128]{0,1:T(8,128)(2,1)S(1)} %bitcast.149), channel_id=1, source_target_pairs={{8,0},{16,8},{24,16},{32,24},{40,32},{48,40},{56,48},{64,56},{72,6... | collective-permute-start | bytes 786440 | tf_op jit(solution)/shard_map/ppermute | solution.py:19
  180.7 4.4 %copy-start.3 = (bf16[8,8,8,128]{3,2,1,0:T(8,128)(2,1)S(1)}, bf16[8,8,8,128]{3,2,1,0:T(8,128)(2,1)}, u32[]{:S(2)}) copy-start(bf16[8,8,8,128]{3,2,1,0:T(8,128)(2,1)} %copy.30) | copy-start | bytes 393220
  185.1 1.6 copy-start.2
Sparse Core Ops, SparseCore 0:
  10.6 36.9 all-gather.1
  58.2 249.6 all-reduce.1
where the time goes:
time: 338 us
  waiting for transfers between devices  153 us (45%)
  blocking collectives  138 us (41%)
  between operations  14.4 us (4%)
  matrix products  10.7 us (3%)
  local copies, waits for them, and re-layouts  8.88 us (3%)
  other arithmetic  8.83 us (3%)
  starting transfers between devices  4.4 us (1%)
    psum x1, waiting for transfers between devices, shards(): lax.psum((partial_sum, jnp.sum(phi_keys, axis=0)), 'dom')  120 us
    psum x1, blocking collectives, shards(): lax.psum((partial_sum, jnp.sum(phi_keys, axis=0)), 'dom')  117 us
    all_gather x1, waiting for transfers between devices, shards(): lax.all_gather(normed, 'head', axis=0, tiled=True)  33 us
    all_to_all x1, blocking collectives, shards(): lax.all_to_all(mixed, 'head', split_axis=0, concat_axis=1, tiled=True)  20.3 us
  transfers between devices with their start and end apart: 4, of which 2 were waited for; matrix products, arithmetic and copies ran while one was open for 6% of the time, Pallas kernels for 0%

commit v1 on v0

v1 whole, which is shorter than its diff:
```python
import functools
import math

import jax
import jax.numpy as jnp
from jax import lax
from jax.experimental import pallas as pl
from jax.experimental.pallas import tpu as pltpu
from jax.sharding import PartitionSpec as P

BLK = 128
NX, NZ, NY = 4, 16, 4
HEADS = 2 * NY
BF16 = jnp.bfloat16
F32 = jnp.float32
MESH = pl.DeviceIdType.MESH
NT = (((1,), (1,)), ((), ()))
NN = (((1,), (0,)), ((), ()))


def mul(a, b, dims=NN):
    return lax.dot_general(a, b, dims, preferred_element_type=F32)


def kernel(
    feats_hbm, gain_ref, w_hbm, wout_hbm, rand_hbm, temper_ref, edge_ref, count_ref, fill_ref,
    out_hbm,
    feats, wout, rand, rot, xg, wt, kv, qq, mkv, mq, phiq, parts, rs, xs, ag, local, mixed,
    ret, outb,
    load_sem, store_sem, x_send, x_recv, w_send, w_recv, n_send, prev_recv, next_recv,
    m_send, mk_recv, mq_recv, rs_send, rs_recv, xs_send, xs_recv, ag_send, ag_recv,
    a_send, a_recv,
):
    dom = lax.axis_index("dom")
    head = lax.axis_index("head")
    y, c = head // 2, head % 2
    x, z = dom // NZ, dom % NZ
    mate = y * 2 + (1 - c)
    n_dom = NX * NZ
    right, left = (dom + 1) % n_dom, (dom + n_dom - 1) % n_dom

    loads = [
        pltpu.make_async_copy(feats_hbm, feats, load_sem.at[0]),
        pltpu.make_async_copy(w_hbm, wt.at[0], load_sem.at[1]),
        pltpu.make_async_copy(rand_hbm, rand, load_sem.at[2]),
        pltpu.make_async_copy(wout_hbm, wout, load_sem.at[3]),
    ]
    for load in loads:
        load.start()

    barrier = pltpu.get_barrier_semaphore()
    friends = [(dom, (head + o) % HEADS) for o in range(1, HEADS)]
    friends += [(d, h) for d in (left, right) for h in (head, mate)]
    friends += [(x * NZ + (z + o) % NZ, head) for o in range(1, NZ)]
    friends += [(((x + o) % NX) * NZ + z, head) for o in range(1, NX)]
    for friend in friends:
        pl.semaphore_signal(barrier, inc=1, device_id=friend, device_id_type=MESH)

    def push(src, dst, send, recv, device):
        copy = pltpu.make_async_remote_copy(
            src_ref=src, dst_ref=dst, send_sem=send, recv_sem=recv,
            device_id=device, device_id_type=MESH,
        )
        copy.start()

    def drain(like, sem):
        pltpu.make_async_copy(like, like, sem).wait()

    loads[0].wait()
    rows = feats[...].astype(F32)
    centred = rows - jnp.mean(rows, axis=-1, keepdims=True)
    spread = jnp.mean(centred * centred, axis=-1, keepdims=True)
    xg[0] = (centred * lax.rsqrt(spread + 1e-05) * gain_ref[...]).astype(BF16)

    loads[1].wait()

    pl.semaphore_wait(barrier, len(friends))
    for o in range(1, NY):
        push(xg.at[0], xg.at[o], x_send, x_recv.at[o - 1], (dom, ((y + o) % NY) * 2 + c))
    push(wt.at[0], wt.at[1], w_send, w_recv, (dom, mate))

    loads[2].wait()
    temper = temper_ref[0]
    scaled = rand[...] * (jnp.sqrt(jnp.full((1, 256), temper, F32)) * 64 ** (-0.25))
    coarse = scaled.astype(BF16).astype(F32)
    rot[...] = jnp.concatenate([coarse, scaled - coarse], axis=0).T.astype(BF16)
    half = temper * (1.0 / 16.0)
    log_root = math.log(16.0)

    drain(wt.at[1], w_recv)
    for o in range(NY):
        if o > 0:
            drain(xg.at[o], x_recv.at[o - 1])
        r = ((y + NY - o) % NY) * 2 + c
        shard = xg[o]
        wq = [wt[i, 0:64] for i in (0, 0, 1, 1)]
        kv2 = mul(jnp.concatenate([wt[0, 64:192], wt[1, 64:192]], axis=0), shard, NT).astype(BF16)
        kv[8 + r] = kv2[0:128]
        mkv[o] = kv2[128:256]
        for d, base in ((right, 0), (left, 16)):
            sem = prev_recv if base == 0 else next_recv
            push(kv.at[8 + r], kv.at[base + r], n_send, sem, (d, head))
        push(mkv.at[o], kv.at[8 + r], m_send, mk_recv, (dom, mate))
        for d, base in ((right, 0), (left, 16)):
            sem = prev_recv if base == 0 else next_recv
            push(mkv.at[o], kv.at[base + r], n_send, sem, (d, mate))
        q2 = mul(shard, jnp.concatenate(wq, axis=0), NT).astype(BF16)
        qq[r] = q2[:, 0:128]
        mq[o] = q2[:, 128:256]
        push(mq.at[o], qq.at[r], m_send, mq_recv, (dom, mate))

    lanes = lax.broadcasted_iota(jnp.int32, (8, 128), 1)[0:1]
    ones16 = jnp.ones((16, 128), BF16)
    rotated = rot[...]

    def key_features(r):
        both = kv[8 + r]
        keys = both[0:64]
        wide = keys.astype(F32)
        norm = jnp.sum(wide * wide, axis=0, keepdims=True)
        lifted = mul(rotated, jnp.concatenate([keys, keys], axis=0))
        phi = jnp.exp(lifted - (norm * half + log_root))
        phi = jnp.where(lanes < fill_ref[dom * 8 + r], phi, 0.0).astype(BF16)
        return phi, jnp.concatenate([ones16, both[64:128]], axis=0)

    drain(kv.at[pl.ds(0, 4)], mk_recv)
    sums = jnp.zeros((80, 256), F32)
    for pair in range(4):
        one, two = key_features(2 * pair), key_features(2 * pair + 1)
        sums += mul(
            jnp.concatenate([one[1], two[1]], axis=1),
            jnp.concatenate([one[0], two[0]], axis=1),
            NT,
        )
    for piece in range(NZ):
        g, j = piece // 2, piece % 2
        parts[piece] = jnp.concatenate(
            [
                sums[16 + 8 * g : 24 + 8 * g, 128 * j : 128 * j + 128],
                sums[0:8, 128 * j : 128 * j + 128],
            ],
            axis=0,
        ).astype(BF16)
    for o in range(1, NZ):
        to = (z + o) % NZ
        push(parts.at[to], rs.at[o - 1], rs_send, rs_recv, (x * NZ + to, head))

    drain(kv.at[pl.ds(0, 4)], mq_recv)
    side = lax.broadcasted_iota(jnp.int32, (128, 128), 1) < 64
    for r in range(8):
        rows_q = qq[r]
        wide = rows_q.astype(F32)
        square = wide * wide
        top = square.astype(BF16)
        rest = (square - top.astype(F32)).astype(BF16)
        norm = mul(ones16, jnp.where(side, top, rest), NT)[0:1]
        lifted = mul(rotated, rows_q, NT)
        phiq[r] = jnp.exp(lifted - (norm * half + log_root)).astype(BF16)

    drain(rs, rs_recv)
    mine = parts[z].astype(F32)
    for o in range(NZ - 1):
        mine += rs[o].astype(F32)
    xs[0] = mine.astype(BF16)
    for o in range(1, NX):
        push(xs.at[0], xs.at[o], xs_send, xs_recv, (((x + o) % NX) * NZ + z, head))

    drain(kv.at[pl.ds(0, 8)], prev_recv)
    drain(kv.at[pl.ds(0, 8)], next_recv)

    def attend(r):
        queries = (qq[r] * 0.125)[:, 0:64]
        scores, values = [], []
        for j in range(6):
            src = edge_ref[r, j]
            block = kv[jnp.clip(src - (dom - 1) * 8, 0, 23)]
            real = jnp.where(j < count_ref[r], fill_ref[src], 0)
            scores.append(jnp.where(lanes < real, mul(queries, block[0:64]), -1e30))
            values.append(jnp.concatenate([ones16, block[64:128]], axis=0))
        top = functools.reduce(jnp.maximum, scores)
        top = jnp.max(top, axis=1, keepdims=True)
        weights = [jnp.exp(s - top).astype(BF16) for s in scores]
        total = mul(jnp.concatenate(values, axis=1), jnp.concatenate(weights, axis=1), NT)
        local[r] = total[16:80] / total[0:1]

    for r in range(4):
        attend(r)

    drain(xs.at[pl.ds(1, 3)], xs_recv)
    for o in range(1, NX):
        mine += xs[o].astype(F32)
    ag[z] = mine.astype(BF16)
    for o in range(1, NZ):
        push(ag.at[z], ag.at[z], ag_send, ag_recv, (x * NZ + (z + o) % NZ, head))

    for r in range(4, 8):
        attend(r)

    drain(ag.at[pl.ds(0, NZ - 1)], ag_recv)
    got = [ag[piece].astype(F32) for piece in range(NZ)]
    stack = [jnp.concatenate([got[0][8:16], got[1][8:16]], axis=1)] * 2
    stack += [
        jnp.concatenate([got[2 * g][0:8], got[2 * g + 1][0:8]], axis=1) for g in range(8)
    ]
    whole = jnp.concatenate(stack, axis=0).astype(BF16)

    def mix(r):
        both = mul(whole, phiq[r])
        return (local[r] + both[16:80] / both[0:1]).astype(BF16)

    ret[head] = mix(head)
    for o in range(1, HEADS):
        to = (head + o) % HEADS
        mixed[o - 1] = mix(to)
        push(mixed.at[o - 1], ret.at[head], a_send, a_recv, (dom, to))
    drain(mixed, a_recv)
    loads[3].wait()
    back = ret[...].reshape(512, 128).T
    outb[...] = mul(back, wout[...]).astype(BF16)
    store = pltpu.make_async_copy(outb, out_hbm, store_sem)
    store.start()

    drain(xg.at[pl.ds(0, 3)], x_send)
    drain(wt.at[0], w_send)
    drain(kv.at[pl.ds(0, 16)], n_send)
    drain(kv.at[pl.ds(0, 8)], m_send)
    drain(rs, rs_send)
    drain(xs.at[pl.ds(1, 3)], xs_send)
    drain(rs, ag_send)
    drain(mixed, a_send)
    store.wait()


def shards(
    node_feats, norm_gain, w_qkv, w_out, rand_feat, temper, edge_src, edge_count, block_fill
):
    any_space = pl.BlockSpec(memory_space=pl.ANY)
    smem = pl.BlockSpec(memory_space=pltpu.SMEM)
    vmem = pl.BlockSpec(memory_space=pltpu.VMEM)
    dma = pltpu.SemaphoreType.DMA
    return pl.pallas_call(
        kernel,
        out_shape=jax.ShapeDtypeStruct(node_feats.shape, BF16),
        in_specs=[any_space, vmem, any_space, any_space, any_space, smem, smem, smem, smem],
        out_specs=any_space,
        scratch_shapes=[
            pltpu.VMEM((128, 512), BF16),
                pltpu.VMEM((512, 512), BF16),
            pltpu.VMEM((64, 256), F32),
            pltpu.VMEM((256, 128), BF16),
            pltpu.VMEM((NY, 128, 512), BF16),
            pltpu.VMEM((2, 192, 512), BF16),
            pltpu.VMEM((24, 128, 128), BF16),
            pltpu.VMEM((8, 128, 128), BF16),
            pltpu.VMEM((NY, 128, 128), BF16),
            pltpu.VMEM((NY, 128, 128), BF16),
            pltpu.VMEM((8, 256, 128), BF16),
            pltpu.VMEM((NZ, 16, 128), BF16),
            pltpu.VMEM((NZ - 1, 16, 128), BF16),
            pltpu.VMEM((NX, 16, 128), BF16),
            pltpu.VMEM((NZ, 16, 128), BF16),
            pltpu.VMEM((8, 64, 128), F32),
            pltpu.VMEM((HEADS - 1, 64, 128), BF16),
            pltpu.VMEM((HEADS, 64, 128), BF16),
            pltpu.VMEM((128, 512), BF16),
            dma((4,)), dma,
            dma, dma((NY - 1,)),
            dma, dma,
            dma, dma, dma,
            dma, dma, dma,
            dma, dma, dma, dma, dma, dma, dma, dma,
        ],
        compiler_params=pltpu.CompilerParams(
            collective_id=0, has_side_effects=True, vmem_limit_bytes=56 * 2**20
        ),
        name="graph_layer",
    )(
        node_feats, norm_gain.reshape(1, -1), w_qkv.T, w_out, rand_feat[0], temper, edge_src,
        edge_count, block_fill,
    )


def solution(mesh):
    return jax.shard_map(
        shards,
        mesh=mesh,
        in_specs=(
            P(("dom", "head"), None),
            P(),
            P(None, "head"),
            P(),
            P("head", None, None),
            P("head"),
            P("dom", None),
            P("dom"),
            P(),
        ),
        out_specs=P(("dom", "head"), None),
        check_vma=False,
    )
```

time: 338 us -> 57.2 us (0.17)
  waiting for transfers between devices: 153 us -> 0 us
  blocking collectives: 138 us -> 0 us
  Pallas kernels: 0 us -> 54.8 us
  between operations: 14.4 us -> 0.66 us
  matrix products: 10.7 us -> 0 us
  other arithmetic: 8.83 us -> 0 us
  local copies, waits for them, and re-layouts: 8.88 us -> 1.57 us
  starting transfers between devices: 4.4 us -> 0 us
    psum x1 -> x0, waiting for transfers between devices: 120 us -> none  [shards(): lax.psum((partial_sum, jnp.sum(phi_keys, axis=0)), 'dom')]
    psum x1 -> x0, blocking collectives: 117 us -> none  [shards(): lax.psum((partial_sum, jnp.sum(phi_keys, axis=0)), 'dom')]
    pallas_call x0 -> x1, Pallas kernels: none -> 54.8 us  [shards(): pl.pallas_call(kernel, out_shape=jax.ShapeDtypeStruct(node_feats.shape, B...]
    all_gather x1 -> x0, waiting for transfers between devices: 33 us -> none  [shards(): lax.all_gather(normed, 'head', axis=0, tiled=True)]
    all_to_all x1 -> x0, blocking collectives: 20.3 us -> none  [shards(): lax.all_to_all(mixed, 'head', split_axis=0, concat_axis=1, tiled=True)]
    dot_general x9 -> x0, matrix products: 10.7 us -> none  [the longest x2 2.38 us: features(): jnp.einsum('nhd,hdm->nhm', scaled, directions, precision=lax.Precision.HI...]
    ppermute x2 -> x0, starting transfers between devices: 4.32 us -> none  [the longest x1 3.02 us: padded(): lax.ppermute(lax.slice_in_dim(block, block.shape[dim] - width, None, axis...]
  transfers between devices with their start and end apart: 4 -> 0, of which waited for: 2 -> 0; matrix products, arithmetic and copies ran while one was open for 6% -> 0% of each run, Pallas kernels for 0% -> 0%
where the time goes in v1:
time: 57.2 us; the launch traced here: 57 us
  Pallas kernels  54.8 us (96%)
  local copies, waits for them, and re-layouts  1.57 us (3%)
  between operations  0.66 us (1%)
    pallas_call x1, Pallas kernels, shards(): pl.pallas_call(kernel, out_shape=jax.ShapeDtypeStruct(node_feats.shape, B...  54.8 us
    unnamed x1, local copies, waits for them, and re-layouts  1.57 us

profile of v1, /device:TPU:1, one launch (start us, length us, event | category | flops | bytes accessed | tf_op | source)
XLA Modules:
  0.0 57.0 jit_solution(13200335704067198944)
XLA Ops:
  0.7 54.8 %graph_layer.1 = bf16[128,512]{1,0:T(8,128)(2,1)} custom-call(bf16[128,512]{1,0:T(8,128)(2,1)} %feats_hbm.1, f32[1,512]{1,0:T(1,128)} %bitcast.5, bf16[192,512]{1,0:T(8,128)(2,1)} %bitcast.3, bf16[512,512]{1,0:T(8,128)(2,1)} %wout_hbm.1, f32[64,256]{1,0:T(8,128)} %bitcast.4, f32[1]{0:T(128)S(6)} %copy.11.temper_ref, s32[8,6]{1,0:T(8,128)} %edge_ref.1, ...), custom_call_target="tpu_custom_call" | custom-call | tf_op jit(solution)/shard_map/graph_layer/pallas_call | solution.py:241
  55.4 1.6 %copy.12 = bf16[128,512]{1,0:T(8,128)(2,1)} copy(bf16[128,512]{1,0:T(8,128)(2,1)} %graph_layer.1) | data formatting | bytes 262144

commit v2 on v1

--- a/solution.py
+++ b/solution.py
@@ -10,6 +10,8 @@
 
 BLK = 128
 NX, NZ, NY = 4, 16, 4
+QUAD = 4
+CUBE = NX * QUAD
 HEADS = 2 * NY
 BF16 = jnp.bfloat16
 F32 = jnp.float32
@@ -51,8 +53,16 @@
     barrier = pltpu.get_barrier_semaphore()
     friends = [(dom, (head + o) % HEADS) for o in range(1, HEADS)]
     friends += [(d, h) for d in (left, right) for h in (head, mate)]
-    friends += [(x * NZ + (z + o) % NZ, head) for o in range(1, NZ)]
-    friends += [(((x + o) % NX) * NZ + z, head) for o in range(1, NX)]
+    quad, low = z // QUAD, z % QUAD
+    place = x * QUAD + low
+    near = []
+    for i in range(NX):
+        for j in range(QUAD):
+            if i or j:
+                nx, nlow = (x + i) % NX, (low + j) % QUAD
+                near.append((nx * QUAD + nlow, (nx * NZ + quad * QUAD + nlow, head)))
+    far = [(x * NZ + (z + QUAD * o) % NZ, head) for o in (2, 1, 3)]
+    friends += [device for _, device in near] + far
     for friend in friends:
         pl.semaphore_signal(barrier, inc=1, device_id=friend, device_id_type=MESH)
 
@@ -86,28 +96,6 @@
     rot[...] = jnp.concatenate([coarse, scaled - coarse], axis=0).T.astype(BF16)
     half = temper * (1.0 / 16.0)
     log_root = math.log(16.0)
-
-    drain(wt.at[1], w_recv)
-    for o in range(NY):
-        if o > 0:
-            drain(xg.at[o], x_recv.at[o - 1])
-        r = ((y + NY - o) % NY) * 2 + c
-        shard = xg[o]
-        wq = [wt[i, 0:64] for i in (0, 0, 1, 1)]
-        kv2 = mul(jnp.concatenate([wt[0, 64:192], wt[1, 64:192]], axis=0), shard, NT).astype(BF16)
-        kv[8 + r] = kv2[0:128]
-        mkv[o] = kv2[128:256]
-        for d, base in ((right, 0), (left, 16)):
-            sem = prev_recv if base == 0 else next_recv
-            push(kv.at[8 + r], kv.at[base + r], n_send, sem, (d, head))
-        push(mkv.at[o], kv.at[8 + r], m_send, mk_recv, (dom, mate))
-        for d, base in ((right, 0), (left, 16)):
-            sem = prev_recv if base == 0 else next_recv
-            push(mkv.at[o], kv.at[base + r], n_send, sem, (d, mate))
-        q2 = mul(shard, jnp.concatenate(wq, axis=0), NT).astype(BF16)
-        qq[r] = q2[:, 0:128]
-        mq[o] = q2[:, 128:256]
-        push(mq.at[o], qq.at[r], m_send, mq_recv, (dom, mate))
 
     lanes = lax.broadcasted_iota(jnp.int32, (8, 128), 1)[0:1]
     ones16 = jnp.ones((16, 128), BF16)
@@ -123,16 +111,35 @@
         phi = jnp.where(lanes < fill_ref[dom * 8 + r], phi, 0.0).astype(BF16)
         return phi, jnp.concatenate([ones16, both[64:128]], axis=0)
 
-    drain(kv.at[pl.ds(0, 4)], mk_recv)
-    sums = jnp.zeros((80, 256), F32)
-    for pair in range(4):
-        one, two = key_features(2 * pair), key_features(2 * pair + 1)
-        sums += mul(
+    def pair_sums(o):
+        drain(mkv.at[o], mk_recv.at[o])
+        first = ((y + NY - o) % NY) * 2
+        one, two = key_features(first), key_features(first + 1)
+        return mul(
             jnp.concatenate([one[1], two[1]], axis=1),
             jnp.concatenate([one[0], two[0]], axis=1),
             NT,
         )
-    for piece in range(NZ):
+
+    drain(wt.at[1], w_recv)
+    order = (0, 1, 3, 2)
+    sums = jnp.zeros((80, 256), F32)
+    for n, o in enumerate(order):
+        if o > 0:
+            drain(xg.at[o], x_recv.at[o - 1])
+        r = ((y + NY - o) % NY) * 2 + c
+        wkv = jnp.concatenate([wt[0, 64:192], wt[1, 64:192]], axis=0)
+        kv2 = mul(wkv, xg[o], NT).astype(BF16)
+        mkv[o] = kv2[128:256]
+        push(mkv.at[o], kv.at[8 + r], m_send, mk_recv.at[o], (dom, mate))
+        kv[8 + r] = kv2[0:128]
+        for d, base, sem in ((right, 0, prev_recv), (left, 16, next_recv)):
+            push(kv.at[8 + r], kv.at[base + r], n_send, sem, (d, head))
+            push(mkv.at[o], kv.at[base + r], n_send, sem, (d, mate))
+        if n > 0:
+            sums += pair_sums(order[n - 1])
+    sums += pair_sums(order[-1])
+    for piece in range(CUBE):
         g, j = piece // 2, piece % 2
         parts[piece] = jnp.concatenate(
             [
@@ -141,13 +148,19 @@
             ],
             axis=0,
         ).astype(BF16)
-    for o in range(1, NZ):
-        to = (z + o) % NZ
-        push(parts.at[to], rs.at[o - 1], rs_send, rs_recv, (x * NZ + to, head))
-
-    drain(kv.at[pl.ds(0, 4)], mq_recv)
+    for slot, (to, device) in enumerate(near):
+        push(parts.at[to], rs.at[slot], rs_send, rs_recv, device)
+
+    wq = jnp.concatenate([wt[i, 0:64] for i in (0, 0, 1, 1)], axis=0)
+    for o in order:
+        r = ((y + NY - o) % NY) * 2 + c
+        q2 = mul(xg[o], wq, NT).astype(BF16)
+        mq[o] = q2[:, 128:256]
+        push(mq.at[o], qq.at[r], m_send, mq_recv, (dom, mate))
+        qq[r] = q2[:, 0:128]
     side = lax.broadcasted_iota(jnp.int32, (128, 128), 1) < 64
-    for r in range(8):
+
+    def query_features(r):
         rows_q = qq[r]
         wide = rows_q.astype(F32)
         square = wide * wide
@@ -157,13 +170,19 @@
         lifted = mul(rotated, rows_q, NT)
         phiq[r] = jnp.exp(lifted - (norm * half + log_root)).astype(BF16)
 
+    for i in range(NY):
+        query_features(2 * i + c)
+    drain(mkv, mq_recv)
+    for i in range(NY):
+        query_features(2 * i + (1 - c))
+
     drain(rs, rs_recv)
-    mine = parts[z].astype(F32)
-    for o in range(NZ - 1):
+    mine = parts[place].astype(F32)
+    for o in range(CUBE - 1):
         mine += rs[o].astype(F32)
     xs[0] = mine.astype(BF16)
-    for o in range(1, NX):
-        push(xs.at[0], xs.at[o], xs_send, xs_recv, (((x + o) % NX) * NZ + z, head))
+    for slot, device in enumerate(far):
+        push(xs.at[0], xs.at[1 + slot], xs_send, xs_recv, device)
 
     drain(kv.at[pl.ds(0, 8)], prev_recv)
     drain(kv.at[pl.ds(0, 8)], next_recv)
@@ -189,15 +208,15 @@
     drain(xs.at[pl.ds(1, 3)], xs_recv)
     for o in range(1, NX):
         mine += xs[o].astype(F32)
-    ag[z] = mine.astype(BF16)
-    for o in range(1, NZ):
-        push(ag.at[z], ag.at[z], ag_send, ag_recv, (x * NZ + (z + o) % NZ, head))
+    ag[place] = mine.astype(BF16)
+    for _, device in near:
+        push(ag.at[place], ag.at[place], ag_send, ag_recv, device)
 
     for r in range(4, 8):
         attend(r)
 
-    drain(ag.at[pl.ds(0, NZ - 1)], ag_recv)
-    got = [ag[piece].astype(F32) for piece in range(NZ)]
+    drain(ag.at[pl.ds(0, CUBE - 1)], ag_recv)
+    got = [ag[piece].astype(F32) for piece in range(CUBE)]
     stack = [jnp.concatenate([got[0][8:16], got[1][8:16]], axis=1)] * 2
     stack += [
         jnp.concatenate([got[2 * g][0:8], got[2 * g + 1][0:8]], axis=1) for g in range(8)
@@ -255,10 +274,10 @@
             pltpu.VMEM((NY, 128, 128), BF16),
             pltpu.VMEM((NY, 128, 128), BF16),
             pltpu.VMEM((8, 256, 128), BF16),
-            pltpu.VMEM((NZ, 16, 128), BF16),
-            pltpu.VMEM((NZ - 1, 16, 128), BF16),
+            pltpu.VMEM((CUBE, 16, 128), BF16),
+            pltpu.VMEM((CUBE - 1, 16, 128), BF16),
             pltpu.VMEM((NX, 16, 128), BF16),
-            pltpu.VMEM((NZ, 16, 128), BF16),
+            pltpu.VMEM((CUBE, 16, 128), BF16),
             pltpu.VMEM((8, 64, 128), F32),
             pltpu.VMEM((HEADS - 1, 64, 128), BF16),
             pltpu.VMEM((HEADS, 64, 128), BF16),
@@ -267,7 +286,7 @@
             dma, dma((NY - 1,)),
             dma, dma,
             dma, dma, dma,
-            dma, dma, dma,
+            dma, dma((NY,)), dma,
             dma, dma, dma, dma, dma, dma, dma, dma,
         ],
         compiler_params=pltpu.CompilerParams(

time: 57.2 us -> 52.2 us (0.913)
  Pallas kernels: 54.8 us -> 49.8 us
    pallas_call x1, Pallas kernels: 54.8 us -> 49.8 us  [shards(): pl.pallas_call(kernel, out_shape=jax.ShapeDtypeStruct(node_feats.shape, B...]
where the time goes in v2:
time: 52.2 us; the launch traced here: 52 us
  Pallas kernels  49.8 us (95%)
  local copies, waits for them, and re-layouts  1.57 us (3%)
  between operations  0.66 us (1%)
    pallas_call x1, Pallas kernels, shards(): pl.pallas_call(kernel, out_shape=jax.ShapeDtypeStruct(node_feats.shape, B...  49.8 us
    unnamed x1, local copies, waits for them, and re-layouts  1.57 us

profile of v2, /device:TPU:1, one launch (start us, length us, event | category | flops | bytes accessed | tf_op | source)
XLA Modules:
  0.0 52.0 jit_solution(10642537048074949006)
XLA Ops:
  0.7 49.8 %graph_layer.1 = bf16[128,512]{1,0:T(8,128)(2,1)} custom-call(bf16[128,512]{1,0:T(8,128)(2,1)} %feats_hbm.1, f32[1,512]{1,0:T(1,128)} %bitcast.5, bf16[192,512]{1,0:T(8,128)(2,1)} %bitcast.3, bf16[512,512]{1,0:T(8,128)(2,1)} %wout_hbm.1, f32[64,256]{1,0:T(8,128)} %bitcast.4, f32[1]{0:T(128)S(6)} %copy.11.temper_ref, s32[8,6]{1,0:T(8,128)} %edge_ref.1, ...), custom_call_target="tpu_custom_call" | custom-call | tf_op jit(solution)/shard_map/graph_layer/pallas_call | solution.py:260
  50.4 1.6 %copy.12 = bf16[128,512]{1,0:T(8,128)(2,1)} copy(bf16[128,512]{1,0:T(8,128)(2,1)} %graph_layer.1) | data formatting | bytes 262144

commit v3 on v2

--- a/solution.py
+++ b/solution.py
@@ -25,11 +25,10 @@
 
 
 def kernel(
-    feats_hbm, gain_ref, w_hbm, wout_hbm, rand_hbm, temper_ref, edge_ref, count_ref, fill_ref,
-    out_hbm,
-    feats, wout, rand, rot, xg, wt, kv, qq, mkv, mq, phiq, parts, rs, xs, ag, local, mixed,
-    ret, outb,
-    load_sem, store_sem, x_send, x_recv, w_send, w_recv, n_send, prev_recv, next_recv,
+    feats_hbm, gain_hbm, w_hbm, rand_hbm, temper_hbm, edge_hbm, count_hbm, fill_hbm,
+    ret,
+    gain, temper_ref, edge_ref, count_ref, fill_ref, feats, rand, rot, xg, wt, kv, qq, mkv, mq, phiq, parts, rs, xs, ag, local, mixed,
+    load_sem, x_send, x_recv, w_send, w_recv, n_send, prev_recv, next_recv,
     m_send, mk_recv, mq_recv, rs_send, rs_recv, xs_send, xs_recv, ag_send, ag_recv,
     a_send, a_recv,
 ):
@@ -45,14 +44,14 @@
         pltpu.make_async_copy(feats_hbm, feats, load_sem.at[0]),
         pltpu.make_async_copy(w_hbm, wt.at[0], load_sem.at[1]),
         pltpu.make_async_copy(rand_hbm, rand, load_sem.at[2]),
-        pltpu.make_async_copy(wout_hbm, wout, load_sem.at[3]),
+        pltpu.make_async_copy(gain_hbm, gain, load_sem.at[3]),
+        pltpu.make_async_copy(temper_hbm, temper_ref, load_sem.at[4]),
+        pltpu.make_async_copy(edge_hbm, edge_ref, load_sem.at[5]),
+        pltpu.make_async_copy(count_hbm, count_ref, load_sem.at[6]),
+        pltpu.make_async_copy(fill_hbm, fill_ref, load_sem.at[7]),
     ]
-    for load in loads:
-        load.start()
-
     barrier = pltpu.get_barrier_semaphore()
-    friends = [(dom, (head + o) % HEADS) for o in range(1, HEADS)]
-    friends += [(d, h) for d in (left, right) for h in (head, mate)]
+    friends = [(d, h) for d in (left, right) for h in (head, mate)]
     quad, low = z // QUAD, z % QUAD
     place = x * QUAD + low
     near = []
@@ -62,9 +61,12 @@
                 nx, nlow = (x + i) % NX, (low + j) % QUAD
                 near.append((nx * QUAD + nlow, (nx * NZ + quad * QUAD + nlow, head)))
     far = [(x * NZ + (z + QUAD * o) % NZ, head) for o in (2, 1, 3)]
-    friends += [device for _, device in near] + far
+    friends = far + friends + [(dom, (head + o) % HEADS) for o in range(1, HEADS)] + [device for _, device in near]
     for friend in friends:
         pl.semaphore_signal(barrier, inc=1, device_id=friend, device_id_type=MESH)
+
+    for load in loads:
+        load.start()
 
     def push(src, dst, send, recv, device):
         copy = pltpu.make_async_remote_copy(
@@ -77,10 +79,11 @@
         pltpu.make_async_copy(like, like, sem).wait()
 
     loads[0].wait()
+    loads[3].wait()
     rows = feats[...].astype(F32)
     centred = rows - jnp.mean(rows, axis=-1, keepdims=True)
     spread = jnp.mean(centred * centred, axis=-1, keepdims=True)
-    xg[0] = (centred * lax.rsqrt(spread + 1e-05) * gain_ref[...]).astype(BF16)
+    xg[0] = (centred * lax.rsqrt(spread + 1e-05) * gain[...]).astype(BF16)
 
     loads[1].wait()
 
@@ -90,8 +93,10 @@
     push(wt.at[0], wt.at[1], w_send, w_recv, (dom, mate))
 
     loads[2].wait()
-    temper = temper_ref[0]
-    scaled = rand[...] * (jnp.sqrt(jnp.full((1, 256), temper, F32)) * 64 ** (-0.25))
+    for i in range(4, 8):
+        loads[i].wait()
+    temper = temper_ref[...]
+    scaled = rand[...] * (jnp.sqrt(temper) * 64 ** (-0.25))
     coarse = scaled.astype(BF16).astype(F32)
     rot[...] = jnp.concatenate([coarse, scaled - coarse], axis=0).T.astype(BF16)
     half = temper * (1.0 / 16.0)
@@ -120,6 +125,13 @@
             jnp.concatenate([one[0], two[0]], axis=1),
             NT,
         )
+
+
+    def share(o):
+        r = ((y + NY - o) % NY) * 2 + c
+        for d, base, sem in ((right, 0, prev_recv), (left, 16, next_recv)):
+            push(kv.at[8 + r], kv.at[base + r], n_send, sem, (d, head))
+            push(mkv.at[o], kv.at[base + r], n_send, sem, (d, mate))
 
     drain(wt.at[1], w_recv)
     order = (0, 1, 3, 2)
@@ -133,9 +145,8 @@
         mkv[o] = kv2[128:256]
         push(mkv.at[o], kv.at[8 + r], m_send, mk_recv.at[o], (dom, mate))
         kv[8 + r] = kv2[0:128]
-        for d, base, sem in ((right, 0, prev_recv), (left, 16, next_recv)):
-            push(kv.at[8 + r], kv.at[base + r], n_send, sem, (d, head))
-            push(mkv.at[o], kv.at[base + r], n_send, sem, (d, mate))
+        if n < 3:
+            share(o)
         if n > 0:
             sums += pair_sums(order[n - 1])
     sums += pair_sums(order[-1])
@@ -150,6 +161,7 @@
         ).astype(BF16)
     for slot, (to, device) in enumerate(near):
         push(parts.at[to], rs.at[slot], rs_send, rs_recv, device)
+    share(order[-1])
 
     wq = jnp.concatenate([wt[i, 0:64] for i in (0, 0, 1, 1)], axis=0)
     for o in order:
@@ -227,17 +239,12 @@
         both = mul(whole, phiq[r])
         return (local[r] + both[16:80] / both[0:1]).astype(BF16)
 
-    ret[head] = mix(head)
-    for o in range(1, HEADS):
-        to = (head + o) % HEADS
+    for o in (4, 5, 2, 3, 6, 7, 1):
+        to = head ^ o
         mixed[o - 1] = mix(to)
         push(mixed.at[o - 1], ret.at[head], a_send, a_recv, (dom, to))
+    ret[head] = mix(head)
     drain(mixed, a_recv)
-    loads[3].wait()
-    back = ret[...].reshape(512, 128).T
-    outb[...] = mul(back, wout[...]).astype(BF16)
-    store = pltpu.make_async_copy(outb, out_hbm, store_sem)
-    store.start()
 
     drain(xg.at[pl.ds(0, 3)], x_send)
     drain(wt.at[0], w_send)
@@ -247,25 +254,25 @@
     drain(xs.at[pl.ds(1, 3)], xs_send)
     drain(rs, ag_send)
     drain(mixed, a_send)
-    store.wait()
 
 
 def shards(
     node_feats, norm_gain, w_qkv, w_out, rand_feat, temper, edge_src, edge_count, block_fill
 ):
-    any_space = pl.BlockSpec(memory_space=pl.ANY)
-    smem = pl.BlockSpec(memory_space=pltpu.SMEM)
-    vmem = pl.BlockSpec(memory_space=pltpu.VMEM)
     dma = pltpu.SemaphoreType.DMA
-    return pl.pallas_call(
+    back = pl.pallas_call(
         kernel,
-        out_shape=jax.ShapeDtypeStruct(node_feats.shape, BF16),
-        in_specs=[any_space, vmem, any_space, any_space, any_space, smem, smem, smem, smem],
-        out_specs=any_space,
+        out_shape=pltpu.VMEM((HEADS, 64, 128), BF16),
+        in_specs=[pl.BlockSpec(memory_space=pltpu.HBM)] * 8,
+        out_specs=pl.BlockSpec(memory_space=pltpu.VMEM),
         scratch_shapes=[
+            pltpu.VMEM((1, 512), F32),
+            pltpu.VMEM((1, 1), F32),
+            pltpu.SMEM((8, 6), jnp.int32),
+            pltpu.SMEM((8,), jnp.int32),
+            pltpu.SMEM((512,), jnp.int32),
             pltpu.VMEM((128, 512), BF16),
-                pltpu.VMEM((512, 512), BF16),
-            pltpu.VMEM((64, 256), F32),
+                pltpu.VMEM((64, 256), F32),
             pltpu.VMEM((256, 128), BF16),
             pltpu.VMEM((NY, 128, 512), BF16),
             pltpu.VMEM((2, 192, 512), BF16),
@@ -280,9 +287,7 @@
             pltpu.VMEM((CUBE, 16, 128), BF16),
             pltpu.VMEM((8, 64, 128), F32),
             pltpu.VMEM((HEADS - 1, 64, 128), BF16),
-            pltpu.VMEM((HEADS, 64, 128), BF16),
-            pltpu.VMEM((128, 512), BF16),
-            dma((4,)), dma,
+            dma((8,)),
             dma, dma((NY - 1,)),
             dma, dma,
             dma, dma, dma,
@@ -294,9 +299,12 @@
         ),
         name="graph_layer",
     )(
-        node_feats, norm_gain.reshape(1, -1), w_qkv.T, w_out, rand_feat[0], temper, edge_src,
+        node_feats, norm_gain.reshape(1, -1), w_qkv.T, rand_feat[0], temper.reshape(1, 1), edge_src,
         edge_count, block_fill,
     )
+    return lax.dot_general(
+        back.reshape(512, 128), w_out, (((0,), (0,)), ((), ())), preferred_element_type=F32
+    ).astype(BF16)
 
 
 def solution(mesh):

time: 52.2 us -> 49 us (0.939)
  Pallas kernels: 49.8 us -> 47.2 us
  local copies, waits for them, and re-layouts: 1.57 us -> 0.01 us
  matrix products: 0 us -> 0.91 us
    pallas_call x1, Pallas kernels: 49.8 us -> 47.2 us  [shards(): pl.pallas_call(kernel, out_shape=pltpu.VMEM((HEADS, 64, 128), BF16), in_s...]
    unnamed x1 -> x2, local copies, waits for them, and re-layouts: 1.57 us -> 0.01 us
    dot_general x0 -> x1, matrix products: none -> 0.91 us  [shards(): lax.dot_general(back.reshape(512, 128), w_out, (((0,), (0,)), ((), ())),...]
where the time goes in v3:
time: 49 us; the launch traced here: 48.9 us
  Pallas kernels  47.2 us (96%)
  matrix products  0.91 us (2%)
  between operations  0.73 us (1%)
    pallas_call x1, Pallas kernels, shards(): pl.pallas_call(kernel, out_shape=pltpu.VMEM((HEADS, 64, 128), BF16), in_s...  47.2 us

profile of v3, /device:TPU:1, one launch (start us, length us, event | category | flops | bytes accessed | tf_op | source)
XLA Modules:
  0.0 48.9 jit_solution(16889438724202272500)
XLA Ops:
  0.0 0.0 copy-start
  0.7 47.2 %graph_layer.1 = bf16[8,64,128]{2,1,0:T(8,128)(2,1)S(1)} custom-call(bf16[128,512]{1,0:T(8,128)(2,1)} %feats_hbm.1, f32[1,512]{1,0:T(1,128)} %bitcast.11, bf16[192,512]{1,0:T(8,128)(2,1)} %bitcast.9, f32[64,256]{1,0:T(8,128)} %bitcast.10, f32[1,1]{1,0:T(1,128)} %bitcast.7.temper_hbm, s32[8,6]{1,0:T(8,128)} %edge_hbm.1, s32[8]{0:T(128)} %count_hbm.1, s32[512]{0:T(512)} %fill_hbm.1), custom_call_target="tpu_custom_call" | custom-call | tf_op jit(solution)/shard_map/graph_layer/pallas_call | solution.py:263
  47.9 0.0 copy-done
  48.0 0.9 %convolution_convert_fusion = bf16[128,512]{1,0:T(8,128)(2,1)} fusion(bf16[512,128]{1,0:T(8,128)(2,1)S(1)} %bitcast.8, bf16[512,512]{1,0:T(8,128)(2,1)S(1)} %copy-done), kind=kOutput, calls=%fused_computation | convolution fusion | flops 67174400 | bytes 786432 | tf_op jit(solution)/shard_map/dot_general | solution.py:305
Async XLA Ops:
  0.0 48.0 %copy-start = (bf16[512,512]{1,0:T(8,128)(2,1)S(1)}, bf16[512,512]{1,0:T(8,128)(2,1)}, u32[]{:S(2)}) copy-start(bf16[512,512]{1,0:T(8,128)(2,1)} %param.12) | copy-start | bytes 1572868

commit v4 on v3

--- a/solution.py
+++ b/solution.py
@@ -12,6 +12,7 @@
 NX, NZ, NY = 4, 16, 4
 QUAD = 4
 CUBE = NX * QUAD
+PARTS = 8
 HEADS = 2 * NY
 BF16 = jnp.bfloat16
 F32 = jnp.float32
@@ -27,7 +28,7 @@
 def kernel(
     feats_hbm, gain_hbm, w_hbm, rand_hbm, temper_hbm, edge_hbm, count_hbm, fill_hbm,
     ret,
-    gain, temper_ref, edge_ref, count_ref, fill_ref, feats, rand, rot, xg, wt, kv, qq, mkv, mq, phiq, parts, rs, xs, ag, local, mixed,
+    gain, temper_ref, edge_ref, count_ref, fill_ref, feats, rand, rot, xg, wt, kv, qq, mkv, mq, phiq, parts, rs, xs, ag, tally, local, mixed,
     load_sem, x_send, x_recv, w_send, w_recv, n_send, prev_recv, next_recv,
     m_send, mk_recv, mq_recv, rs_send, rs_recv, xs_send, xs_recv, ag_send, ag_recv,
     a_send, a_recv,
@@ -54,14 +55,16 @@
     friends = [(d, h) for d in (left, right) for h in (head, mate)]
     quad, low = z // QUAD, z % QUAD
     place = x * QUAD + low
-    near = []
-    for i in range(NX):
-        for j in range(QUAD):
-            if i or j:
-                nx, nlow = (x + i) % NX, (low + j) % QUAD
-                near.append((nx * QUAD + nlow, (nx * NZ + quad * QUAD + nlow, head)))
+    middle = (low + 1) // 2 == 1
+    own = x * 2 + (low + 1) % 2
+    near = [
+        (((x + i) % NX) * NZ + quad * QUAD + (low + j) % QUAD, head)
+        for i in (2, 1, 3, 0)
+        for j in (3, 1, 2, 0)
+        if i or j
+    ]
     far = [(x * NZ + (z + QUAD * o) % NZ, head) for o in (2, 1, 3)]
-    friends = far + friends + [(dom, (head + o) % HEADS) for o in range(1, HEADS)] + [device for _, device in near]
+    friends = far + [(dom, head ^ o) for o in (4, 5, 2, 3, 6, 7, 1)] + friends + near
     for friend in friends:
         pl.semaphore_signal(barrier, inc=1, device_id=friend, device_id_type=MESH)
 
@@ -77,6 +80,27 @@
 
     def drain(like, sem):
         pltpu.make_async_copy(like, like, sem).wait()
+
+    def thin(ref, i):
+        return ref.at[i, pl.ds(0, 16)]
+
+    def either(wide, ref, start, count, sem):
+        @pl.when(wide)
+        def _():
+            drain(ref.at[pl.ds(start, count)], sem)
+
+        @pl.when(jnp.logical_not(wide))
+        def _():
+            drain(ref.at[pl.ds(start, count), pl.ds(0, 16)], sem)
+
+    def fan(ref, here, there, send, recv, device):
+        @pl.when(x == 0)
+        def _():
+            push(ref.at[here], ref.at[there], send, recv, device)
+
+        @pl.when(x > 0)
+        def _():
+            push(thin(ref, here), thin(ref, there), send, recv, device)
 
     loads[0].wait()
     loads[3].wait()
@@ -137,6 +161,8 @@
     order = (0, 1, 3, 2)
     sums = jnp.zeros((80, 256), F32)
     for n, o in enumerate(order):
+        if n == 3:
+            sums += pair_sums(order[2])
         if o > 0:
             drain(xg.at[o], x_recv.at[o - 1])
         r = ((y + NY - o) % NY) * 2 + c
@@ -147,20 +173,36 @@
         kv[8 + r] = kv2[0:128]
         if n < 3:
             share(o)
-        if n > 0:
+        if n in (1, 2):
             sums += pair_sums(order[n - 1])
     sums += pair_sums(order[-1])
-    for piece in range(CUBE):
-        g, j = piece // 2, piece % 2
-        parts[piece] = jnp.concatenate(
-            [
-                sums[16 + 8 * g : 24 + 8 * g, 128 * j : 128 * j + 128],
-                sums[0:8, 128 * j : 128 * j + 128],
-            ],
-            axis=0,
-        ).astype(BF16)
-    for slot, (to, device) in enumerate(near):
-        push(parts.at[to], rs.at[slot], rs_send, rs_recv, device)
+    rounded = sums.astype(BF16)
+    for k in range(PARTS):
+        g, columns = k // 2, slice(128 * (k % 2), 128 * (k % 2) + 128)
+        parts[k, 0:16] = rounded[16 + 16 * g : 32 + 16 * g, columns]
+        parts[k, 16:32] = rounded[0:16, columns]
+
+    @pl.when(middle)
+    def _():
+        rs[place] = parts[own]
+
+    for i in (2, 1, 3, 0):
+        for j in (1, 2):
+            to = (x + i) % NX
+
+            @pl.when((low != j) if i == 0 else (low >= 0))
+            def _():
+                device = (to * NZ + quad * QUAD + j, head)
+                part = to * 2 + j - 1
+
+                @pl.when(to == 0)
+                def _():
+                    push(parts.at[part], rs.at[place], rs_send, rs_recv, device)
+
+                @pl.when(to > 0)
+                def _():
+                    push(thin(parts, part), thin(rs, place), rs_send, rs_recv, device)
+
     share(order[-1])
 
     wq = jnp.concatenate([wt[i, 0:64] for i in (0, 0, 1, 1)], axis=0)
@@ -188,13 +230,12 @@
     for i in range(NY):
         query_features(2 * i + (1 - c))
 
-    drain(rs, rs_recv)
-    mine = parts[place].astype(F32)
-    for o in range(CUBE - 1):
-        mine += rs[o].astype(F32)
-    xs[0] = mine.astype(BF16)
-    for slot, device in enumerate(far):
-        push(xs.at[0], xs.at[1 + slot], xs_send, xs_recv, device)
+    @pl.when(middle)
+    def _():
+        either(x == 0, rs, 0, CUBE - 1, rs_recv)
+        xs[0] = sum(rs[i].astype(F32) for i in range(CUBE)).astype(BF16)
+        for slot, device in enumerate(far):
+            fan(xs, 0, 1 + slot, xs_send, xs_recv, device)
 
     drain(kv.at[pl.ds(0, 8)], prev_recv)
     drain(kv.at[pl.ds(0, 8)], next_recv)
@@ -217,23 +258,26 @@
     for r in range(4):
         attend(r)
 
-    drain(xs.at[pl.ds(1, 3)], xs_recv)
-    for o in range(1, NX):
-        mine += xs[o].astype(F32)
-    ag[place] = mine.astype(BF16)
-    for _, device in near:
-        push(ag.at[place], ag.at[place], ag_send, ag_recv, device)
+    @pl.when(middle)
+    def _():
+        either(x == 0, xs, 1, 3, xs_recv)
+        ag[own] = sum(xs[i].astype(F32) for i in range(4)).astype(BF16)
+        for device in near:
+            fan(ag, own, own, ag_send, ag_recv, device)
 
     for r in range(4, 8):
         attend(r)
 
-    drain(ag.at[pl.ds(0, CUBE - 1)], ag_recv)
-    got = [ag[piece].astype(F32) for piece in range(CUBE)]
-    stack = [jnp.concatenate([got[0][8:16], got[1][8:16]], axis=1)] * 2
-    stack += [
-        jnp.concatenate([got[2 * g][0:8], got[2 * g + 1][0:8]], axis=1) for g in range(8)
-    ]
-    whole = jnp.concatenate(stack, axis=0).astype(BF16)
+    one, two = jnp.logical_and(middle, x > 0), jnp.logical_and(middle, x == 0)
+    for case, count in ((jnp.logical_not(middle), 10), (one, 9), (two, 8)):
+
+        @pl.when(case)
+        def _():
+            drain(tally.at[pl.ds(0, count)], ag_recv)
+
+    stack = [jnp.concatenate([ag[0, 16:32], ag[1, 16:32]], axis=1)]
+    stack += [jnp.concatenate([ag[2 * g, 0:16], ag[2 * g + 1, 0:16]], axis=1) for g in range(4)]
+    whole = jnp.concatenate(stack, axis=0)
 
     def mix(r):
         both = mul(whole, phiq[r])
@@ -250,9 +294,18 @@
     drain(wt.at[0], w_send)
     drain(kv.at[pl.ds(0, 16)], n_send)
     drain(kv.at[pl.ds(0, 8)], m_send)
-    drain(rs, rs_send)
-    drain(xs.at[pl.ds(1, 3)], xs_send)
-    drain(rs, ag_send)
+
+    @pl.when(middle)
+    def _():
+        either(x == 0, xs, 1, 3, xs_send)
+        either(x == 0, rs, 0, CUBE - 1, ag_send)
+
+    for case, count in ((jnp.logical_not(middle), 10), (one, 9), (two, 8)):
+
+        @pl.when(case)
+        def _():
+            drain(tally.at[pl.ds(0, count)], rs_send)
+
     drain(mixed, a_send)
 
 
@@ -281,10 +334,11 @@
             pltpu.VMEM((NY, 128, 128), BF16),
             pltpu.VMEM((NY, 128, 128), BF16),
             pltpu.VMEM((8, 256, 128), BF16),
-            pltpu.VMEM((CUBE, 16, 128), BF16),
-            pltpu.VMEM((CUBE - 1, 16, 128), BF16),
-            pltpu.VMEM((NX, 16, 128), BF16),
-            pltpu.VMEM((CUBE, 16, 128), BF16),
+            pltpu.VMEM((PARTS, 32, 128), BF16),
+            pltpu.VMEM((CUBE, 32, 128), BF16),
+            pltpu.VMEM((4, 32, 128), BF16),
+            pltpu.VMEM((PARTS, 32, 128), BF16),
+            pltpu.VMEM((10, 16, 128), BF16),
             pltpu.VMEM((8, 64, 128), F32),
             pltpu.VMEM((HEADS - 1, 64, 128), BF16),
             dma((8,)),

time: 49 us -> 48.2 us (0.984)
  Pallas kernels: 47.2 us -> 46.4 us
    pallas_call x1, Pallas kernels: 47.2 us -> 46.4 us  [shards(): pl.pallas_call(kernel, out_shape=pltpu.VMEM((HEADS, 64, 128), BF16), in_s...]
where the time goes in v4:
time: 48.2 us; the launch traced here: 48.1 us
  Pallas kernels  46.4 us (96%)
  matrix products  0.91 us (2%)
  between operations  0.73 us (2%)
    pallas_call x1, Pallas kernels, shards(): pl.pallas_call(kernel, out_shape=pltpu.VMEM((HEADS, 64, 128), BF16), in_s...  46.4 us

profile of v4, /device:TPU:1, one launch (start us, length us, event | category | flops | bytes accessed | tf_op | source)
XLA Modules:
  0.0 48.1 jit_solution(15241371909566574704)
XLA Ops:
  0.0 0.0 copy-start
  0.7 46.4 %graph_layer.1 = bf16[8,64,128]{2,1,0:T(8,128)(2,1)S(1)} custom-call(bf16[128,512]{1,0:T(8,128)(2,1)} %feats_hbm.1, f32[1,512]{1,0:T(1,128)} %bitcast.11, bf16[192,512]{1,0:T(8,128)(2,1)} %bitcast.9, f32[64,256]{1,0:T(8,128)} %bitcast.10, f32[1,1]{1,0:T(1,128)} %bitcast.7.temper_hbm, s32[8,6]{1,0:T(8,128)} %edge_hbm.1, s32[8]{0:T(128)} %count_hbm.1, s32[512]{0:T(512)} %fill_hbm.1), custom_call_target="tpu_custom_call" | custom-call | tf_op jit(solution)/shard_map/graph_layer/pallas_call | solution.py:316
  47.1 0.0 copy-done
  47.2 0.9 %convolution_convert_fusion = bf16[128,512]{1,0:T(8,128)(2,1)} fusion(bf16[512,128]{1,0:T(8,128)(2,1)S(1)} %bitcast.8, bf16[512,512]{1,0:T(8,128)(2,1)S(1)} %copy-done), kind=kOutput, calls=%fused_computation | convolution fusion | flops 67174400 | bytes 786432 | tf_op jit(solution)/shard_map/dot_general | solution.py:359
Async XLA Ops:
  0.0 47.2 %copy-start = (bf16[512,512]{1,0:T(8,128)(2,1)S(1)}, bf16[512,512]{1,0:T(8,128)(2,1)}, u32[]{:S(2)}) copy-start(bf16[512,512]{1,0:T(8,128)(2,1)} %param.12) | copy-start | bytes 1572868

commit v5 on v4

--- a/solution.py
+++ b/solution.py
@@ -141,9 +141,10 @@
         return phi, jnp.concatenate([ones16, both[64:128]], axis=0)
 
     def pair_sums(o):
+        first = ((y + NY - o) % NY) * 2
+        one = key_features(first + c)
         drain(mkv.at[o], mk_recv.at[o])
-        first = ((y + NY - o) % NY) * 2
-        one, two = key_features(first), key_features(first + 1)
+        two = key_features(first + 1 - c)
         return mul(
             jnp.concatenate([one[1], two[1]], axis=1),
             jnp.concatenate([one[0], two[0]], axis=1),
@@ -262,8 +263,13 @@
     def _():
         either(x == 0, xs, 1, 3, xs_recv)
         ag[own] = sum(xs[i].astype(F32) for i in range(4)).astype(BF16)
-        for device in near:
-            fan(ag, own, own, ag_send, ag_recv, device)
+        for j in range(QUAD):
+            for i in (2, 1, 3, 0):
+
+                @pl.when((low != j) if i == 0 else (low >= 0))
+                def _():
+                    device = (((x + i) % NX) * NZ + quad * QUAD + j, head)
+                    fan(ag, own, own, ag_send, ag_recv, device)
 
     for r in range(4, 8):
         attend(r)
@@ -283,12 +289,18 @@
         both = mul(whole, phiq[r])
         return (local[r] + both[16:80] / both[0:1]).astype(BF16)
 
-    for o in (4, 5, 2, 3, 6, 7, 1):
-        to = head ^ o
-        mixed[o - 1] = mix(to)
-        push(mixed.at[o - 1], ret.at[head], a_send, a_recv, (dom, to))
-    ret[head] = mix(head)
-    drain(mixed, a_recv)
+    for to in (1, 0, 3, 2, 5, 4, 7, 6):
+
+        @pl.when(head == to)
+        def _():
+            ret[to] = mix(to)
+
+        @pl.when(head != to)
+        def _():
+            mixed[to] = mix(to)
+            push(mixed.at[to], ret.at[head], a_send, a_recv, (dom, to))
+
+    drain(mixed.at[pl.ds(0, HEADS - 1)], a_recv)
 
     drain(xg.at[pl.ds(0, 3)], x_send)
     drain(wt.at[0], w_send)
@@ -306,7 +318,7 @@
         def _():
             drain(tally.at[pl.ds(0, count)], rs_send)
 
-    drain(mixed, a_send)
+    drain(mixed.at[pl.ds(0, HEADS - 1)], a_send)
 
 
 def shards(
@@ -340,7 +352,7 @@
             pltpu.VMEM((PARTS, 32, 128), BF16),
             pltpu.VMEM((10, 16, 128), BF16),
             pltpu.VMEM((8, 64, 128), F32),
-            pltpu.VMEM((HEADS - 1, 64, 128), BF16),
+            pltpu.VMEM((HEADS, 64, 128), BF16),
             dma((8,)),
             dma, dma((NY - 1,)),
             dma, dma,

time: 48.2 us -> 47.8 us (level)
  no operation moved by 1% of the time
where the time goes in v5:
time: 47.8 us; the launch traced here: 47.7 us
  Pallas kernels  46.1 us (96%)
  matrix products  0.91 us (2%)
  between operations  0.73 us (2%)
    pallas_call x1, Pallas kernels, shards(): pl.pallas_call(kernel, out_shape=pltpu.VMEM((HEADS, 64, 128), BF16), in_s...  46.1 us

profile of v5, /device:TPU:1, one launch (start us, length us, event | category | flops | bytes accessed | tf_op | source)
XLA Modules:
  0.0 47.7 jit_solution(10610447673213542627)
XLA Ops:
  0.0 0.0 copy-start
  0.7 46.1 %graph_layer.1 = bf16[8,64,128]{2,1,0:T(8,128)(2,1)S(1)} custom-call(bf16[128,512]{1,0:T(8,128)(2,1)} %feats_hbm.1, f32[1,512]{1,0:T(1,128)} %bitcast.11, bf16[192,512]{1,0:T(8,128)(2,1)} %bitcast.9, f32[64,256]{1,0:T(8,128)} %bitcast.10, f32[1,1]{1,0:T(1,128)} %bitcast.7.temper_hbm, s32[8,6]{1,0:T(8,128)} %edge_hbm.1, s32[8]{0:T(128)} %count_hbm.1, s32[512]{0:T(512)} %fill_hbm.1), custom_call_target="tpu_custom_call" | custom-call | tf_op jit(solution)/shard_map/graph_layer/pallas_call | solution.py:328
  46.8 0.0 copy-done
  46.8 0.9 %convolution_convert_fusion = bf16[128,512]{1,0:T(8,128)(2,1)} fusion(bf16[512,128]{1,0:T(8,128)(2,1)S(1)} %bitcast.8, bf16[512,512]{1,0:T(8,128)(2,1)S(1)} %copy-done), kind=kOutput, calls=%fused_computation | convolution fusion | flops 67174400 | bytes 786432 | tf_op jit(solution)/shard_map/dot_general | solution.py:371
Async XLA Ops:
  0.0 46.8 %copy-start = (bf16[512,512]{1,0:T(8,128)(2,1)S(1)}, bf16[512,512]{1,0:T(8,128)(2,1)}, u32[]{:S(2)}) copy-start(bf16[512,512]{1,0:T(8,128)(2,1)} %param.12) | copy-start | bytes 1572868

commit v6 on v5

--- a/solution.py
+++ b/solution.py
@@ -55,8 +55,8 @@
     friends = [(d, h) for d in (left, right) for h in (head, mate)]
     quad, low = z // QUAD, z % QUAD
     place = x * QUAD + low
-    middle = (low + 1) // 2 == 1
-    own = x * 2 + (low + 1) % 2
+    middle = low < 2
+    own = x * 2 + low % 2
     near = [
         (((x + i) % NX) * NZ + quad * QUAD + (low + j) % QUAD, head)
         for i in (2, 1, 3, 0)
@@ -188,13 +188,13 @@
         rs[place] = parts[own]
 
     for i in (2, 1, 3, 0):
-        for j in (1, 2):
+        for j in (0, 1):
             to = (x + i) % NX
 
             @pl.when((low != j) if i == 0 else (low >= 0))
             def _():
                 device = (to * NZ + quad * QUAD + j, head)
-                part = to * 2 + j - 1
+                part = to * 2 + j
 
                 @pl.when(to == 0)
                 def _():

time: 47.8 us -> 47.3 us (0.990)
  Pallas kernels: 46.1 us -> 45.5 us
    pallas_call x1, Pallas kernels: 46.1 us -> 45.5 us  [shards(): pl.pallas_call(kernel, out_shape=pltpu.VMEM((HEADS, 64, 128), BF16), in_s...]
where the time goes in v6:
time: 47.3 us; the launch traced here: 47.1 us
  Pallas kernels  45.5 us (96%)
  matrix products  0.91 us (2%)
  between operations  0.73 us (2%)
    pallas_call x1, Pallas kernels, shards(): pl.pallas_call(kernel, out_shape=pltpu.VMEM((HEADS, 64, 128), BF16), in_s...  45.5 us

profile of v6, /device:TPU:1, one launch (start us, length us, event | category | flops | bytes accessed | tf_op | source)
XLA Modules:
  0.0 47.1 jit_solution(5703430408890551228)
XLA Ops:
  0.0 0.0 copy-start
  0.7 45.5 %graph_layer.1 = bf16[8,64,128]{2,1,0:T(8,128)(2,1)S(1)} custom-call(bf16[128,512]{1,0:T(8,128)(2,1)} %feats_hbm.1, f32[1,512]{1,0:T(1,128)} %bitcast.11, bf16[192,512]{1,0:T(8,128)(2,1)} %bitcast.9, f32[64,256]{1,0:T(8,128)} %bitcast.10, f32[1,1]{1,0:T(1,128)} %bitcast.7.temper_hbm, s32[8,6]{1,0:T(8,128)} %edge_hbm.1, s32[8]{0:T(128)} %count_hbm.1, s32[512]{0:T(512)} %fill_hbm.1), custom_call_target="tpu_custom_call" | custom-call | tf_op jit(solution)/shard_map/graph_layer/pallas_call | solution.py:328
  46.2 0.0 copy-done
  46.2 0.9 %convolution_convert_fusion = bf16[128,512]{1,0:T(8,128)(2,1)} fusion(bf16[512,128]{1,0:T(8,128)(2,1)S(1)} %bitcast.8, bf16[512,512]{1,0:T(8,128)(2,1)S(1)} %copy-done), kind=kOutput, calls=%fused_computation | convolution fusion | flops 67174400 | bytes 786432 | tf_op jit(solution)/shard_map/dot_general | solution.py:371
Async XLA Ops:
  0.0 46.2 %copy-start = (bf16[512,512]{1,0:T(8,128)(2,1)S(1)}, bf16[512,512]{1,0:T(8,128)(2,1)}, u32[]{:S(2)}) copy-start(bf16[512,512]{1,0:T(8,128)(2,1)} %param.12) | copy-start | bytes 1572868

commit v7 on v6

--- a/solution.py
+++ b/solution.py
@@ -172,7 +172,7 @@
         mkv[o] = kv2[128:256]
         push(mkv.at[o], kv.at[8 + r], m_send, mk_recv.at[o], (dom, mate))
         kv[8 + r] = kv2[0:128]
-        if n < 3:
+        if n < 2:
             share(o)
         if n in (1, 2):
             sums += pair_sums(order[n - 1])
@@ -204,7 +204,8 @@
                 def _():
                     push(thin(parts, part), thin(rs, place), rs_send, rs_recv, device)
 
-    share(order[-1])
+    share(order[2])
+    share(order[3])
 
     wq = jnp.concatenate([wt[i, 0:64] for i in (0, 0, 1, 1)], axis=0)
     for o in order:
@@ -264,11 +265,11 @@
         either(x == 0, xs, 1, 3, xs_recv)
         ag[own] = sum(xs[i].astype(F32) for i in range(4)).astype(BF16)
         for j in range(QUAD):
-            for i in (2, 1, 3, 0):
-
-                @pl.when((low != j) if i == 0 else (low >= 0))
+            for i in range(NX):
+
+                @pl.when(jnp.logical_or(low != j, x != i))
                 def _():
-                    device = (((x + i) % NX) * NZ + quad * QUAD + j, head)
+                    device = (i * NZ + quad * QUAD + j, head)
                     fan(ag, own, own, ag_send, ag_recv, device)
 
     for r in range(4, 8):

time: 47.3 us -> 47.2 us (level)
  no operation moved by 1% of the time
where the time goes in v7:
time: 47.2 us; the launch traced here: 47.1 us
  Pallas kernels  45.4 us (96%)
  matrix products  0.91 us (2%)
  between operations  0.73 us (2%)
    pallas_call x1, Pallas kernels, shards(): pl.pallas_call(kernel, out_shape=pltpu.VMEM((HEADS, 64, 128), BF16), in_s...  45.4 us

profile of v7, /device:TPU:1, one launch (start us, length us, event | category | flops | bytes accessed | tf_op | source)
XLA Modules:
  0.0 47.1 jit_solution(16544141116938153426)
XLA Ops:
  0.0 0.0 copy-start
  0.7 45.4 %graph_layer.1 = bf16[8,64,128]{2,1,0:T(8,128)(2,1)S(1)} custom-call(bf16[128,512]{1,0:T(8,128)(2,1)} %feats_hbm.1, f32[1,512]{1,0:T(1,128)} %bitcast.11, bf16[192,512]{1,0:T(8,128)(2,1)} %bitcast.9, f32[64,256]{1,0:T(8,128)} %bitcast.10, f32[1,1]{1,0:T(1,128)} %bitcast.7.temper_hbm, s32[8,6]{1,0:T(8,128)} %edge_hbm.1, s32[8]{0:T(128)} %count_hbm.1, s32[512]{0:T(512)} %fill_hbm.1), custom_call_target="tpu_custom_call" | custom-call | tf_op jit(solution)/shard_map/graph_layer/pallas_call | solution.py:329
  46.2 0.0 copy-done
  46.2 0.9 %convolution_convert_fusion = bf16[128,512]{1,0:T(8,128)(2,1)} fusion(bf16[512,128]{1,0:T(8,128)(2,1)S(1)} %bitcast.8, bf16[512,512]{1,0:T(8,128)(2,1)S(1)} %copy-done), kind=kOutput, calls=%fused_computation | convolution fusion | flops 67174400 | bytes 786432 | tf_op jit(solution)/shard_map/dot_general | solution.py:372
Async XLA Ops:
  0.0 46.2 %copy-start = (bf16[512,512]{1,0:T(8,128)(2,1)S(1)}, bf16[512,512]{1,0:T(8,128)(2,1)}, u32[]{:S(2)}) copy-start(bf16[512,512]{1,0:T(8,128)(2,1)} %param.12) | copy-start | bytes 1572868
